TPU v7x, 256 devices: a whole 4x4x8 slice. The times are simulated.
256 devices in a mesh: grp: 8 (over z), leaf: 32 (over y, x, core).
Axes of the slice: x: 4, y: 4, z: 8, core: 2. Of those that a mesh axis runs over, the one named last changes fastest.
Arguments:
- configs: bfloat16 [524288, 64], P(('grp', 'leaf')), may hold values from -6 to 6, as said below
- order: int32 [256, 2048], P(('grp', 'leaf')), may hold values from 0 to 2047, each once within a row
- w_in: bfloat16 [64, 128], replicated, may hold values from -0.75 to 0.75
- bias_in: float32 [128], replicated, may hold values from -3 to 3
- w_out: bfloat16 [128, 128], replicated, may hold values from -0.5 to 0.5
- noise: float32 [524288], P(('grp', 'leaf')), may hold values from 0.2 to 2
- right_side: float32 [524288], P(('grp', 'leaf')), may hold values from -12 to 12, as said below
- near_blocks: int32 [2048, 6], P(('grp', 'leaf')), may hold values from 0 to 255
- near_live: int32 [2048, 6], P(('grp', 'leaf')), may hold values 0 or 1
- skeleton: int32 [8, 256], P('grp'), may hold values from 0 to 65535
Outputs:
- solution: float32 [524288], P(('grp', 'leaf'))
- residual: float32 [524288], P(('grp', 'leaf'))
Inputs may be any that keep to these rules, and one draw needn't show every extreme that they name: `configs`: configurations of order one. `right_side`: targets of order one.
All inputs are finite; a program needn't handle non-finite values. No bound on the sum of `near_live` on one device may be relied on, other than what follows from the above.
Results may differ from a plain program's by a relative error of at most 0.039.
Values may be sent and summed in bfloat16 or wider, within the bound.
A program may use at most 128 MiB of HBM per device.

v0:
```python
import jax
import jax.numpy as jnp
from jax import lax
from jax.sharding import PartitionSpec as P

BLK = 256
NEAR = 6
ITERS = 4
sharpness = 10.0
highest = lax.Precision.HIGHEST


def kernel_rows(left, right):
    inner = lax.dot_general(
        left, right, (((1,), (1,)), ((), ())), preferred_element_type=jnp.float32
    )
    return jnp.exp(sharpness * (inner - 1.0))


def features_of(inputs, w_in, bias_in, w_out):
    hidden = jnp.tanh(jnp.dot(inputs, w_in, preferred_element_type=jnp.float32) + bias_in).astype(
        jnp.bfloat16
    )
    raw = jnp.dot(hidden, w_out, preferred_element_type=jnp.float32)
    return (raw * lax.rsqrt(jnp.sum(raw * raw, -1, keepdims=True) + 1e-06)).astype(jnp.bfloat16)


def near_tiles(inputs):
    own_feat, part_feat, own_vec, part_vec, weights, out_weight = inputs
    self_tile = kernel_rows(own_feat, own_feat)
    cross = jnp.exp(
        sharpness
        * (jnp.einsum("if,kjf->kij", own_feat, part_feat, preferred_element_type=jnp.float32) - 1.0)
    )
    partner_tile = jnp.exp(
        sharpness
        * (
            jnp.einsum("kif,kjf->kij", part_feat, part_feat, preferred_element_type=jnp.float32)
            - 1.0
        )
    )
    own_out = out_weight * jnp.dot(self_tile, own_vec, precision=highest)
    own_out = own_out + jnp.sum(
        weights[:, None] * jnp.einsum("kij,kj->ki", cross, part_vec, precision=highest), 0
    )
    back = jnp.einsum("kij,i->kj", cross, own_vec, precision=highest) + jnp.einsum(
        "kij,kj->ki", partner_tile, part_vec, precision=highest
    )
    return (own_out, weights[:, None] * back)


def on_device(
    configs, order, w_in, bias_in, w_out, noise, right_side, near_blocks, near_live, skeleton
):
    row_count = configs.shape[0]
    blocks_dev = row_count // BLK
    tree_rows = jnp.take(configs, order[0], axis=0)
    own_features = features_of(tree_rows, w_in, bias_in, w_out)
    group_feat = lax.all_gather(own_features, "leaf", axis=0, tiled=True)
    group_blocks = group_feat.shape[0] // BLK
    skel_feat = jnp.take(group_feat, skeleton[0], axis=0)
    all_skel = lax.all_gather(skel_feat, "grp", axis=0, tiled=True)
    basis = kernel_rows(own_features, skel_feat)
    coupling = kernel_rows(skel_feat, all_skel)
    live_mask = near_live.astype(jnp.float32)
    out_weights = jnp.sum(live_mask, 1)
    flat_partners = near_blocks.reshape(-1)
    part_feat = jnp.take(group_feat.reshape(group_blocks, BLK, -1), flat_partners, axis=0).reshape(
        blocks_dev, NEAR, BLK, -1
    )
    own_blocks = own_features.reshape(blocks_dev, BLK, -1)
    picker = (jnp.arange(group_blocks, dtype=jnp.int32)[:, None] == flat_partners[None, :]).astype(
        jnp.float32
    )
    precond = 1.0 / (1.0 + noise)
    solution = jnp.zeros_like(right_side)
    residual = right_side

    def inner_total(left, right):
        return lax.psum(jnp.sum(left * right), ("grp", "leaf"))

    scaled = residual * precond
    direction = scaled
    product_now = inner_total(residual, scaled)
    for step in range(ITERS):
        whole = lax.all_gather(direction, "leaf", axis=0, tiled=True)
        part_vec = jnp.take(whole.reshape(group_blocks, BLK), near_blocks, axis=0)
        own_out, back = lax.map(
            near_tiles,
            (
                own_blocks,
                part_feat,
                direction.reshape(blocks_dev, BLK),
                part_vec,
                live_mask,
                out_weights,
            ),
        )
        back_flat = back.reshape(-1, BLK)
        returned = lax.psum_scatter(
            jnp.dot(picker, back_flat, precision=highest).astype(jnp.bfloat16),
            "leaf",
            scatter_dimension=0,
            tiled=True,
        ).astype(jnp.float32)
        apply_local_charge = jnp.dot(direction, basis, precision=highest)
        group_total = lax.psum(apply_local_charge, "leaf")
        charges = lax.all_gather(group_total[None, :], "grp", axis=0, tiled=True)
        field = jnp.dot(coupling, charges.reshape(-1), precision=highest)
        far_part = jnp.dot(basis, field, precision=highest)
        image = (own_out + returned).reshape(-1) + far_part + noise * direction
        step_size = product_now / inner_total(direction, image)
        solution = solution + step_size * direction
        residual = residual - step_size * image
        if step + 1 < ITERS:
            scaled = residual * precond
            product_next = inner_total(residual, scaled)
            direction = scaled + product_next / product_now * direction
            product_now = product_next
    return (solution, residual)


def solution(mesh):
    in_specs = (
        P(("grp", "leaf"), None),
        P(("grp", "leaf"), None),
        P(),
        P(),
        P(),
        P(("grp", "leaf")),
        P(("grp", "leaf")),
        P(("grp", "leaf"), None),
        P(("grp", "leaf"), None),
        P("grp", None),
    )
    out_specs = (P(("grp", "leaf")), P(("grp", "leaf")))
    return jax.shard_map(
        on_device, mesh=mesh, in_specs=in_specs, out_specs=out_specs, check_vma=False
    )
```

profile of v0, /device:TPU:1, one launch (start us, length us, event | category | flops | bytes accessed | tf_op | source)
XLA Modules:
  0.0 1393.6 jit_solution(11065837192118993395)
XLA Ops:
  9.9 6.2 gather_fusion
  18.3 26.4 %all_gather.31 = f32[65536]{0:T(1024)S(1)} all-gather(f32[2048]{0:T(1024)S(1)} %fusion.156), channel_id=1, replica_groups=mesh['grp'=8,'leaf'=32] {'leaf'}, dimensions={0}, use_global_device_ids=true | all-gather | bytes 270336 | tf_op jit(solution)/shard_map/all_gather | solution.py:86
  45.9 54.2 %all-gather.6.cloned.1.call-done = bf16[65536,128]{1,0:T(8,128)(2,1)} async-done(((bf16[2048,128]{1,0:T(8,128)(2,1)}), bf16[65536,128]{1,0:T(8,128)(2,1)}) %all-gather.6.cloned.1.call-update) | async-done | bytes 16777232 | tf_op jit(solution)/shard_map/all_gather | solution.py:59
  100.1 8.7 gather_fusion.2
  108.9 1.8 fusion.135
  110.7 20.9 %all_gather.32 = bf16[2048,128]{1,0:T(8,128)(2,1)S(1)} all-gather(bf16[256,128]{1,0:T(8,128)(2,1)S(1)} %broadcast_select_fusion.1), channel_id=1, replica_groups=mesh['grp'=8,'leaf'=32] {'grp'}, dimensions={0}, use_global_device_ids=true | all-gather | bytes 589824 | tf_op jit(solution)/shard_map/all_gather | solution.py:62
  131.6 8.5 gather_fusion.1
  140.1 3.9 broadcast_select_fusion
  144.0 71.0 %while.60 = (s32[]{:T(128)}, f32[8,256]{1,0:T(8,128)S(1)}, f32[8,6,256]{2,1,0:T(8,128)S(1)}, f32[8]{0:T(128)S(1)}, bf16[8,256,128]{2,1,0:T(8,128)(2,1)S(1)}, /*i...) while((s32[]{:T(128)}, f32[8,256]{1,0:T(8,128)S(1)}, ...), condition=%wide.region_6.8_spmd, body=%wide.region_4.7_spmd.sunk | while | flops 234756352 | bytes 9386733 | solution.py:88
  149.8 1.6 fusion.307
  158.6 1.6 fusion.307
  167.5 1.6 fusion.307
  176.4 1.6 fusion.307
  194.1 1.6 fusion.307
  203.0 1.6 fusion.307
  211.9 1.6 fusion.307
  216.0 1.8 fusion.133
  218.7 68.3 %psum.85 = f32[1,256]{1,0:T(1,128)S(1)} all-reduce(f32[1,256]{1,0:T(1,128)S(1)} %fusion.159), channel_id=1, replica_groups=mesh['grp'=8,'leaf'=32] {'leaf'}, use_global_device_ids=true, to_apply=%region_8.10 | all-reduce | flops 256 | bytes 2048 | tf_op jit(solution)/shard_map/psum | solution.py:107
  287.1 11.3 all-gather
  298.3 3.3 convolution_bitcast_fusion.3
  301.7 1.9 fusion.160
  304.8 74.9 %all-reduce = (f32[]{:T(128)}, f32[]{:T(128)}) all-reduce(f32[]{:T(128)} %get-tuple-element.568, f32[]{:T(128)} %get-tuple-element.567), channel_id=1, replica_groups=mesh['grp'=8,'leaf'=32] {'grp','leaf'}, use_global_device_ids=true, to_apply=%region_1.2 | all-reduce | flops 2 | bytes 16 | tf_op jit(solution)/shard_map/psum | solution.py:80
  381.7 74.4 %psum.87 = f32[]{:T(128)} all-reduce(f32[]{:T(128)} %get-tuple-element.647), channel_id=1, replica_groups=mesh['grp'=8,'leaf'=32] {'grp','leaf'}, use_global_device_ids=true, to_apply=%region_12.14 | all-reduce | flops 1 | bytes 8 | tf_op jit(solution)/shard_map/psum | solution.py:80
  457.5 25.0 %all_gather.34 = f32[65536]{0:T(1024)S(1)} all-gather(f32[2048]{0:T(1024)S(1)} %multiply_add_fusion.10), channel_id=1, replica_groups=mesh['grp'=8,'leaf'=32] {'leaf'}, dimensions={0}, use_global_device_ids=true | all-gather | bytes 270336 | tf_op jit(solution)/shard_map/all_gather | solution.py:86
  483.3 70.9 %while.61 = (s32[]{:T(128)}, f32[8,256]{1,0:T(8,128)S(1)}, f32[8,6,256]{2,1,0:T(8,128)S(1)}, f32[8]{0:T(128)S(1)}, bf16[8,256,128]{2,1,0:T(8,128)(2,1)S(1)}, /*i...) while((s32[]{:T(128)}, f32[8,256]{1,0:T(8,128)S(1)}, ...), condition=%wide.region_15.17_spmd, body=%wide.region_13.16_spmd.sunk | while | flops 234756352 | bytes 9386733 | solution.py:88
  497.9 1.6 fusion.327
  506.8 1.6 fusion.327
  515.7 1.6 fusion.327
  524.5 1.6 fusion.327
  533.4 1.6 fusion.327
  542.3 1.6 fusion.327
  551.1 1.6 fusion.327
  555.3 2.5 fusion.161
  557.8 62.3 %psum.88 = f32[1,256]{1,0:T(1,128)S(1)} all-reduce(f32[1,256]{1,0:T(1,128)S(1)} %fusion.161), channel_id=1, replica_groups=mesh['grp'=8,'leaf'=32] {'leaf'}, use_global_device_ids=true, to_apply=%region_17.19 | all-reduce | flops 256 | bytes 2048 | tf_op jit(solution)/shard_map/psum | solution.py:107
  620.1 10.8 all-gather.1
  630.9 3.3 convolution_bitcast_fusion.2
  634.2 1.9 fusion.162
  637.4 77.4 %psum.89 = f32[]{:T(128)} all-reduce(f32[]{:T(128)} %multiply_reduce_fusion.5), channel_id=1, replica_groups=mesh['grp'=8,'leaf'=32] {'grp','leaf'}, use_global_device_ids=true, to_apply=%region_19.21 | all-reduce | flops 1 | bytes 8 | tf_op jit(solution)/shard_map/psum | solution.py:80
  716.8 74.3 %psum.90 = f32[]{:T(128)} all-reduce(f32[]{:T(128)} %get-tuple-element.645), channel_id=1, replica_groups=mesh['grp'=8,'leaf'=32] {'grp','leaf'}, use_global_device_ids=true, to_apply=%region_21.23 | all-reduce | flops 1 | bytes 8 | tf_op jit(solution)/shard_map/psum | solution.py:80
  792.5 25.3 %all_gather.36 = f32[65536]{0:T(1024)S(1)} all-gather(f32[2048]{0:T(1024)S(1)} %multiply_add_fusion.8), channel_id=1, replica_groups=mesh['grp'=8,'leaf'=32] {'leaf'}, dimensions={0}, use_global_device_ids=true | all-gather | bytes 270336 | tf_op jit(solution)/shard_map/all_gather | solution.py:86
  818.6 71.0 %while.62 = (s32[]{:T(128)}, f32[8,256]{1,0:T(8,128)S(1)}, f32[8,6,256]{2,1,0:T(8,128)S(1)}, f32[8]{0:T(128)S(1)}, bf16[8,256,128]{2,1,0:T(8,128)(2,1)S(1)}, /*i...) while((s32[]{:T(128)}, f32[8,256]{1,0:T(8,128)S(1)}, ...), condition=%wide.region_24.26_spmd, body=%wide.region_22.25_spmd.sunk | while | flops 234756352 | bytes 9386733 | solution.py:88
  824.3 1.6 fusion.347
  842.1 1.6 fusion.347
  851.0 1.6 fusion.347
  859.8 1.6 fusion.347
  868.7 1.6 fusion.347
  877.6 1.6 fusion.347
  886.4 1.6 fusion.347
  890.6 2.5 fusion.163
  893.1 62.3 %psum.91 = f32[1,256]{1,0:T(1,128)S(1)} all-reduce(f32[1,256]{1,0:T(1,128)S(1)} %fusion.163), channel_id=1, replica_groups=mesh['grp'=8,'leaf'=32] {'leaf'}, use_global_device_ids=true, to_apply=%region_26.28 | all-reduce | flops 256 | bytes 2048 | tf_op jit(solution)/shard_map/psum | solution.py:107
  955.4 10.9 all-gather.2
  966.3 3.3 convolution_bitcast_fusion.1
  969.6 1.9 fusion.164
  972.8 77.3 %psum.92 = f32[]{:T(128)} all-reduce(f32[]{:T(128)} %multiply_reduce_fusion.3), channel_id=1, replica_groups=mesh['grp'=8,'leaf'=32] {'grp','leaf'}, use_global_device_ids=true, to_apply=%region_28.30 | all-reduce | flops 1 | bytes 8 | tf_op jit(solution)/shard_map/psum | solution.py:80
  1052.0 74.3 %psum.93 = f32[]{:T(128)} all-reduce(f32[]{:T(128)} %get-tuple-element.643), channel_id=1, replica_groups=mesh['grp'=8,'leaf'=32] {'grp','leaf'}, use_global_device_ids=true, to_apply=%region_30.32 | all-reduce | flops 1 | bytes 8 | tf_op jit(solution)/shard_map/psum | solution.py:80
  1127.7 25.1 %all_gather.38 = f32[65536]{0:T(1024)S(1)} all-gather(f32[2048]{0:T(1024)S(1)} %multiply_add_fusion.6), channel_id=1, replica_groups=mesh['grp'=8,'leaf'=32] {'leaf'}, dimensions={0}, use_global_device_ids=true | all-gather | bytes 270336 | tf_op jit(solution)/shard_map/all_gather | solution.py:86
  1153.6 70.9 %while.63 = (s32[]{:T(128)}, f32[8,256]{1,0:T(8,128)S(1)}, f32[8,6,256]{2,1,0:T(8,128)S(1)}, f32[8]{0:T(128)S(1)}, bf16[8,256,128]{2,1,0:T(8,128)(2,1)S(1)}, /*i...) while((s32[]{:T(128)}, f32[8,256]{1,0:T(8,128)S(1)}, ...), condition=%wide.region_33.35_spmd, body=%wide.region_31.34_spmd.sunk | while | flops 234756352 | bytes 9386733 | solution.py:88
  1159.3 1.6 fusion.367
  1225.5 2.5 fusion.165
  1228.0 62.4 %psum.94 = f32[1,256]{1,0:T(1,128)S(1)} all-reduce(f32[1,256]{1,0:T(1,128)S(1)} %fusion.165), channel_id=1, replica_groups=mesh['grp'=8,'leaf'=32] {'leaf'}, use_global_device_ids=true, to_apply=%region_35.37 | all-reduce | flops 256 | bytes 2048 | tf_op jit(solution)/shard_map/psum | solution.py:107
  1290.4 10.8 all-gather.3
  1301.2 3.3 convolution_bitcast_fusion
  1304.5 1.9 fusion.166
  1307.7 77.3 %psum.95 = f32[]{:T(128)} all-reduce(f32[]{:T(128)} %multiply_reduce_fusion.1), channel_id=1, replica_groups=mesh['grp'=8,'leaf'=32] {'grp','leaf'}, use_global_device_ids=true, to_apply=%region_37.39 | all-reduce | flops 1 | bytes 8 | tf_op jit(solution)/shard_map/psum | solution.py:80
  (544 shorter events, 267.7 us)
Async XLA Ops:
  7.2 8.9 copy-start
  7.2 92.9 %all-gather.6.cloned.1.call-start = ((), (), s32[]{:S(2)}) async-start(), calls=%async_computation.4 | async-start | bytes 17301504 | tf_op jit(solution)/shard_map/all_gather | solution.py:59
  9.9 6.2 copy-start.11
  9.9 6.2 copy-start.12
  16.8 1.3 copy-start.8
  16.8 1.4 copy-start.6
  16.8 1.4 copy-start.7
  16.8 1.5 copy-start.9
  16.9 28.7 %copy-start.10 = (s32[1,256]{1,0:T(1,128)S(1)}, s32[1,256]{1,0:T(1,128)}, u32[]{:S(2)}) copy-start(s32[1,256]{1,0:T(1,128)} %param.29) | copy-start | bytes 3076
  18.0 90.8 %copy-start.5 = (bf16[2048,128]{1,0:T(8,128)(2,1)S(1)}, bf16[2048,128]{1,0:T(8,128)(2,1)}, u32[]{:S(2)}) copy-start(bf16[2048,128]{1,0:T(8,128)(2,1)} %multiply_convert_fusion) | copy-start | bytes 1572868
  18.0 285.5 %reduce-scatter.5.cloned.1.call-start = ((), (), s32[]{:S(2)}) async-start(), calls=%async_computation.5 | async-start | bytes 135168 | tf_op jit(solution)/shard_map/reduce_scatter | solution.py:100
  215.0 2.8 copy-start.1
  215.9 420.2 %reduce-scatter.7.cloned.1.call-start = ((), (), s32[]{:S(2)}) async-start(), calls=%async_computation.6 | async-start | bytes 135168 | tf_op jit(solution)/shard_map/reduce_scatter | solution.py:100
  555.2 416.3 %reduce-scatter.9.cloned.1.call-start = ((), (), s32[]{:S(2)}) async-start(), calls=%async_computation.7 | async-start | bytes 135168 | tf_op jit(solution)/shard_map/reduce_scatter | solution.py:100
  557.8 76.5 %copy-start.2 = (f32[2048,256]{1,0:T(8,128)S(1)}, f32[2048,256]{1,0:T(8,128)}, u32[]{:S(2)}) copy-start(f32[2048,256]{1,0:T(8,128)} %fusion.135) | copy-start | bytes 6291460
  890.5 415.9 %reduce-scatter.11.cloned.1.call-start = ((), (), s32[]{:S(2)}) async-start(), calls=%async_computation.8 | async-start | bytes 135168 | tf_op jit(solution)/shard_map/reduce_scatter | solution.py:100
  893.1 76.5 %copy-start.3 = (f32[2048,256]{1,0:T(8,128)S(1)}, f32[2048,256]{1,0:T(8,128)}, u32[]{:S(2)}) copy-start(f32[2048,256]{1,0:T(8,128)} %fusion.135) | copy-start | bytes 6291460
  1228.0 76.5 %copy-start.4 = (f32[2048,256]{1,0:T(8,128)S(1)}, f32[2048,256]{1,0:T(8,128)}, u32[]{:S(2)}) copy-start(f32[2048,256]{1,0:T(8,128)} %fusion.135) | copy-start | bytes 6291460
Sparse Core Ops, SparseCore 0:
  18.2 81.8 all-gather.5
  216.1 82.5 reduce-scatter.4
  555.3 74.3 reduce-scatter.6
  890.6 74.4 reduce-scatter.8
  1225.6 74.4 reduce-scatter.10
where the time goes:
time: 1400 us; the launch traced here: 1390 us
  blocking collectives  952 us (68%)
  matrix products  271 us (19%)
  waiting for transfers between devices  54.3 us (4%)
  local copies, waits for them, and re-layouts  50.2 us (4%)
  other arithmetic  40.6 us (3%)
  between operations  23.8 us (2%)
    psum x7, blocking collectives, inner_total(): return lax.psum(jnp.sum(left * right), ('grp', 'leaf'))  530 us
    psum x4, blocking collectives, on_device(): group_total = lax.psum(apply_local_charge, 'leaf')  255 us
    all_gather x4, blocking collectives, on_device(): whole = lax.all_gather(direction, 'leaf', axis=0, tiled=True)  102 us
    all_gather x1, waiting for transfers between devices, on_device(): group_feat = lax.all_gather(own_features, 'leaf', axis=0, tiled=True)  54.2 us
    dot_general x32, matrix products, near_tiles(): jnp.einsum('kij,kj->ki', partner_tile, part_vec, precision=highest)  51.6 us
    dot_general x32, matrix products, near_tiles(): jnp.einsum('kif,kjf->kij', part_feat, part_feat, preferred_element_type=j...  47.5 us
    dot_general x32, matrix products, near_tiles(): jnp.einsum('kij,i->kj', cross, own_vec, precision=highest)  46.2 us
    dot_general x32, matrix products, near_tiles(): jnp.einsum('if,kjf->kij', own_feat, part_feat, preferred_element_type=jnp...  44.1 us
  transfers between devices with their start and end apart: 5, of which 1 were waited for; matrix products, arithmetic and copies ran while one was open for 2% of the time, Pallas kernels for 0%

commit v1 on v0

--- a/solution.py
+++ b/solution.py
@@ -8,6 +8,28 @@
 ITERS = 4
 sharpness = 10.0
 highest = lax.Precision.HIGHEST
+
+
+def in_order(blocks, dim):
+    blocks = jnp.moveaxis(blocks, 0, dim)
+    dims = blocks.shape
+    return blocks.reshape(*dims[:dim], dims[dim] * dims[dim + 1], *dims[dim + 2 :])
+
+
+def grow_blocks(x, axis):
+    length = lax.axis_size(axis)
+    tiles = x[None]
+    for level in range(length.bit_length() - 1):
+        distance = 1 << level
+        other = lax.ppermute(tiles, axis, [(i, i ^ distance) for i in range(length)])
+        both = jnp.stack([tiles, other])
+        upper = lax.axis_index(axis) >> level & 1
+        tiles = jnp.where(upper == 0, both, both[::-1]).reshape(-1, *x.shape)
+    return tiles
+
+
+def doubled_up(array, axis, dim):
+    return in_order(grow_blocks(array, axis), dim)
 
 
 def kernel_rows(left, right):
@@ -56,7 +78,7 @@
     blocks_dev = row_count // BLK
     tree_rows = jnp.take(configs, order[0], axis=0)
     own_features = features_of(tree_rows, w_in, bias_in, w_out)
-    group_feat = lax.all_gather(own_features, "leaf", axis=0, tiled=True)
+    group_feat = doubled_up(own_features, "leaf", 0)
     group_blocks = group_feat.shape[0] // BLK
     skel_feat = jnp.take(group_feat, skeleton[0], axis=0)
     all_skel = lax.all_gather(skel_feat, "grp", axis=0, tiled=True)

time: 1400 us -> 1740 us (1.24)
  blocking collectives: 952 us -> 1140 us
  waiting for transfers between devices: 54.3 us -> 163 us
  other arithmetic: 40.6 us -> 82.4 us
    all_gather x4, blocking collectives: 102 us -> 284 us  [on_device(): whole = lax.all_gather(direction, 'leaf', axis=0, tiled=True)]
    ppermute x0 -> x5, waiting for transfers between devices: none -> 162 us  [grow_blocks(): lax.ppermute(tiles, axis, [(i, i ^ distance) for i in range(length)])]
    all_gather x1 -> x0, waiting for transfers between devices: 54.2 us -> none  [on_device(): group_feat = lax.all_gather(own_features, 'leaf', axis=0, tiled=True)]
    select_n x0 -> x4, other arithmetic: none -> 22.7 us  [grow_blocks(): tiles = jnp.where(upper == 0, both, both[::-1]).reshape(-1, *x.shape)]
    another operation x0 -> x7, other arithmetic: none -> 19.6 us  [grow_blocks(): both = jnp.stack([tiles, other])]
  transfers between devices with their start and end apart: 5 -> 9, of which waited for: 1 -> 4; matrix products, arithmetic and copies ran while one was open for 2% -> 2% of each run, Pallas kernels for 0% -> 0%
where the time goes in v1:
time: 1740 us; the launch traced here: 1730 us
  blocking collectives  1140 us (66%)
  matrix products  272 us (16%)
  waiting for transfers between devices  163 us (9%)
  other arithmetic  82.4 us (5%)
  local copies, waits for them, and re-layouts  50.2 us (3%)
  between operations  24.1 us (1%)
    psum x7, blocking collectives, inner_total(): return lax.psum(jnp.sum(left * right), ('grp', 'leaf'))  529 us
    all_gather x4, blocking collectives, on_device(): whole = lax.all_gather(direction, 'leaf', axis=0, tiled=True)  284 us
    psum x4, blocking collectives, on_device(): group_total = lax.psum(apply_local_charge, 'leaf')  254 us
    ppermute x5, waiting for transfers between devices, grow_blocks(): lax.ppermute(tiles, axis, [(i, i ^ distance) for i in range(length)])  162 us
    dot_general x32, matrix products, near_tiles(): jnp.einsum('kij,kj->ki', partner_tile, part_vec, precision=highest)  51.6 us
    dot_general x32, matrix products, near_tiles(): jnp.einsum('kif,kjf->kij', part_feat, part_feat, preferred_element_type=j...  47.6 us
    dot_general x32, matrix products, near_tiles(): jnp.einsum('kij,i->kj', cross, own_vec, precision=highest)  46.2 us
    all_gather x4, blocking collectives, on_device(): charges = lax.all_gather(group_total[None, :], 'grp', axis=0, tiled=True)  44.9 us
  transfers between devices with their start and end apart: 9, of which 4 were waited for; matrix products, arithmetic and copies ran while one was open for 2% of the time, Pallas kernels for 0%

profile of v1, /device:TPU:1, one launch (start us, length us, event | category | flops | bytes accessed | tf_op | source)
XLA Modules:
  0.0 1734.0 jit_solution(1515968757438981289)
XLA Ops:
  9.9 6.2 gather_fusion
  17.2 3.3 collective-permute-start
  22.5 24.5 %collective-permute-done.1 = bf16[2,2048,128]{2,1,0:T(8,128)(2,1)} collective-permute-done((bf16[2,2048,128]{2,1,0:T(8,128)(2,1)S(1)}, bf16[2,2048,128]{2,1,0:T(8,128)(2,1)}, u32[]{:S(2)}, u32[]{:S(2)}) %collective-permute-start.1) | collective-permute-done | bytes 1048608 | tf_op jit(solution)/shard_map/ppermute | solution.py:24
  49.9 46.5 %collective-permute-done.2 = bf16[4,2048,128]{2,1,0:T(8,128)(2,1)} collective-permute-done((bf16[4,2048,128]{2,1,0:T(8,128)(2,1)S(1)}, bf16[4,2048,128]{2,1,0:T(8,128)(2,1)}, u32[]{:S(2)}, u32[]{:S(2)}) %collective-permute-start.2) | collective-permute-done | bytes 2097184 | tf_op jit(solution)/shard_map/ppermute | solution.py:24
  96.4 2.0 pad_maximum_fusion.2
  98.4 2.8 reverse_select_fusion.2
  101.2 90.3 %collective-permute-done.3 = bf16[8,2048,128]{2,1,0:T(8,128)(2,1)} collective-permute-done((bf16[8,2048,128]{2,1,0:T(8,128)(2,1)}, bf16[8,2048,128]{2,1,0:T(8,128)(2,1)}, u32[]{:S(2)}, u32[]{:S(2)}) %collective-permute-start.3) | collective-permute-done | bytes 4194336 | tf_op jit(solution)/shard_map/ppermute | solution.py:24
  191.5 7.5 pad_maximum_fusion.1
  199.0 11.3 reverse_select_fusion.1
  211.6 200.1 %all_gather.27 = f32[65536]{0:T(1024)S(1)} all-gather(f32[2048]{0:T(1024)S(1)} %fusion.158), channel_id=1, replica_groups=mesh['grp'=8,'leaf'=32] {'leaf'}, dimensions={0}, use_global_device_ids=true | all-gather | bytes 270336 | tf_op jit(solution)/shard_map/all_gather | solution.py:108
  413.1 8.0 pad_maximum_fusion
  421.1 8.2 reverse_select_fusion
  429.4 8.5 gather_fusion.1
  437.9 3.9 broadcast_select_fusion
  441.8 8.7 gather_fusion.2
  450.5 23.3 %all_gather.28 = bf16[2048,128]{1,0:T(8,128)(2,1)S(1)} all-gather(bf16[256,128]{1,0:T(8,128)(2,1)S(1)} %broadcast_select_fusion.1), channel_id=1, replica_groups=mesh['grp'=8,'leaf'=32] {'grp'}, dimensions={0}, use_global_device_ids=true | all-gather | bytes 589824 | tf_op jit(solution)/shard_map/all_gather | solution.py:84
  473.8 1.8 fusion.135
  475.6 71.0 %while.60 = (s32[]{:T(128)}, f32[8,256]{1,0:T(8,128)S(1)}, f32[8,6,256]{2,1,0:T(8,128)S(1)}, f32[8]{0:T(128)S(1)}, bf16[8,256,128]{2,1,0:T(8,128)(2,1)S(1)}, /*i...) while((s32[]{:T(128)}, f32[8,256]{1,0:T(8,128)S(1)}, ...), condition=%wide.region_6.8_spmd, body=%wide.region_4.7_spmd.sunk | while | flops 234756352 | bytes 9386733 | solution.py:110
  481.4 1.6 fusion.311
  490.2 1.6 fusion.311
  499.1 1.6 fusion.311
  516.8 1.6 fusion.311
  525.7 1.6 fusion.311
  534.6 1.6 fusion.311
  543.5 1.6 fusion.311
  547.6 1.8 fusion.133
  550.3 67.9 %psum.85 = f32[1,256]{1,0:T(1,128)S(1)} all-reduce(f32[1,256]{1,0:T(1,128)S(1)} %fusion.161), channel_id=1, replica_groups=mesh['grp'=8,'leaf'=32] {'leaf'}, use_global_device_ids=true, to_apply=%region_8.10 | all-reduce | flops 256 | bytes 2048 | tf_op jit(solution)/shard_map/psum | solution.py:129
  618.1 12.0 all-gather
  630.2 3.3 convolution_bitcast_fusion.3
  633.5 1.9 fusion.162
  636.7 74.7 %all-reduce = (f32[]{:T(128)}, f32[]{:T(128)}) all-reduce(f32[]{:T(128)} %get-tuple-element.568, f32[]{:T(128)} %get-tuple-element.567), channel_id=1, replica_groups=mesh['grp'=8,'leaf'=32] {'grp','leaf'}, use_global_device_ids=true, to_apply=%region_1.2 | all-reduce | flops 2 | bytes 16 | tf_op jit(solution)/shard_map/psum | solution.py:102
  713.3 74.5 %psum.87 = f32[]{:T(128)} all-reduce(f32[]{:T(128)} %get-tuple-element.647), channel_id=1, replica_groups=mesh['grp'=8,'leaf'=32] {'grp','leaf'}, use_global_device_ids=true, to_apply=%region_12.14 | all-reduce | flops 1 | bytes 8 | tf_op jit(solution)/shard_map/psum | solution.py:102
  789.1 33.4 %all_gather.30 = f32[65536]{0:T(1024)S(1)} all-gather(f32[2048]{0:T(1024)S(1)} %multiply_add_fusion.10), channel_id=1, replica_groups=mesh['grp'=8,'leaf'=32] {'leaf'}, dimensions={0}, use_global_device_ids=true | all-gather | bytes 270336 | tf_op jit(solution)/shard_map/all_gather | solution.py:108
  823.3 71.0 %while.61 = (s32[]{:T(128)}, f32[8,256]{1,0:T(8,128)S(1)}, f32[8,6,256]{2,1,0:T(8,128)S(1)}, f32[8]{0:T(128)S(1)}, bf16[8,256,128]{2,1,0:T(8,128)(2,1)S(1)}, /*i...) while((s32[]{:T(128)}, f32[8,256]{1,0:T(8,128)S(1)}, ...), condition=%wide.region_15.17_spmd, body=%wide.region_13.16_spmd.sunk | while | flops 234756352 | bytes 9386733 | solution.py:110
  837.9 1.6 fusion.331
  846.8 1.6 fusion.331
  864.5 1.6 fusion.331
  873.4 1.6 fusion.331
  882.3 1.6 fusion.331
  891.1 1.6 fusion.331
  895.3 2.7 fusion.163
  898.0 62.2 %psum.88 = f32[1,256]{1,0:T(1,128)S(1)} all-reduce(f32[1,256]{1,0:T(1,128)S(1)} %fusion.163), channel_id=1, replica_groups=mesh['grp'=8,'leaf'=32] {'leaf'}, use_global_device_ids=true, to_apply=%region_17.19 | all-reduce | flops 256 | bytes 2048 | tf_op jit(solution)/shard_map/psum | solution.py:129
  960.1 11.1 all-gather.1
  971.2 3.3 convolution_bitcast_fusion.2
  974.6 1.9 fusion.164
  977.7 77.1 %psum.89 = f32[]{:T(128)} all-reduce(f32[]{:T(128)} %multiply_reduce_fusion.5), channel_id=1, replica_groups=mesh['grp'=8,'leaf'=32] {'grp','leaf'}, use_global_device_ids=true, to_apply=%region_19.21 | all-reduce | flops 1 | bytes 8 | tf_op jit(solution)/shard_map/psum | solution.py:102
  1056.7 74.3 %psum.90 = f32[]{:T(128)} all-reduce(f32[]{:T(128)} %get-tuple-element.645), channel_id=1, replica_groups=mesh['grp'=8,'leaf'=32] {'grp','leaf'}, use_global_device_ids=true, to_apply=%region_21.23 | all-reduce | flops 1 | bytes 8 | tf_op jit(solution)/shard_map/psum | solution.py:102
  1132.4 25.1 %all_gather.32 = f32[65536]{0:T(1024)S(1)} all-gather(f32[2048]{0:T(1024)S(1)} %multiply_add_fusion.8), channel_id=1, replica_groups=mesh['grp'=8,'leaf'=32] {'leaf'}, dimensions={0}, use_global_device_ids=true | all-gather | bytes 270336 | tf_op jit(solution)/shard_map/all_gather | solution.py:108
  1158.4 71.0 %while.62 = (s32[]{:T(128)}, f32[8,256]{1,0:T(8,128)S(1)}, f32[8,6,256]{2,1,0:T(8,128)S(1)}, f32[8]{0:T(128)S(1)}, bf16[8,256,128]{2,1,0:T(8,128)(2,1)S(1)}, /*i...) while((s32[]{:T(128)}, f32[8,256]{1,0:T(8,128)S(1)}, ...), condition=%wide.region_24.26_spmd, body=%wide.region_22.25_spmd.sunk | while | flops 234756352 | bytes 9386733 | solution.py:110
  1230.4 2.7 fusion.165
  1233.0 62.2 %psum.91 = f32[1,256]{1,0:T(1,128)S(1)} all-reduce(f32[1,256]{1,0:T(1,128)S(1)} %fusion.165), channel_id=1, replica_groups=mesh['grp'=8,'leaf'=32] {'leaf'}, use_global_device_ids=true, to_apply=%region_26.28 | all-reduce | flops 256 | bytes 2048 | tf_op jit(solution)/shard_map/psum | solution.py:129
  1295.3 11.1 all-gather.2
  1306.3 3.3 convolution_bitcast_fusion.1
  1309.7 1.9 fusion.166
  1312.8 77.1 %psum.92 = f32[]{:T(128)} all-reduce(f32[]{:T(128)} %multiply_reduce_fusion.3), channel_id=1, replica_groups=mesh['grp'=8,'leaf'=32] {'grp','leaf'}, use_global_device_ids=true, to_apply=%region_28.30 | all-reduce | flops 1 | bytes 8 | tf_op jit(solution)/shard_map/psum | solution.py:102
  1391.9 74.3 %psum.93 = f32[]{:T(128)} all-reduce(f32[]{:T(128)} %get-tuple-element.643), channel_id=1, replica_groups=mesh['grp'=8,'leaf'=32] {'grp','leaf'}, use_global_device_ids=true, to_apply=%region_30.32 | all-reduce | flops 1 | bytes 8 | tf_op jit(solution)/shard_map/psum | solution.py:102
  1467.6 25.2 %all_gather.34 = f32[65536]{0:T(1024)S(1)} all-gather(f32[2048]{0:T(1024)S(1)} %multiply_add_fusion.6), channel_id=1, replica_groups=mesh['grp'=8,'leaf'=32] {'leaf'}, dimensions={0}, use_global_device_ids=true | all-gather | bytes 270336 | tf_op jit(solution)/shard_map/all_gather | solution.py:108
  1493.5 71.0 %while.63 = (s32[]{:T(128)}, f32[8,256]{1,0:T(8,128)S(1)}, f32[8,6,256]{2,1,0:T(8,128)S(1)}, f32[8]{0:T(128)S(1)}, bf16[8,256,128]{2,1,0:T(8,128)(2,1)S(1)}, /*i...) while((s32[]{:T(128)}, f32[8,256]{1,0:T(8,128)S(1)}, ...), condition=%wide.region_33.35_spmd, body=%wide.region_31.34_spmd.sunk | while | flops 234756352 | bytes 9386733 | solution.py:110
  1565.5 2.7 fusion.167
  1568.1 62.2 %psum.94 = f32[1,256]{1,0:T(1,128)S(1)} all-reduce(f32[1,256]{1,0:T(1,128)S(1)} %fusion.167), channel_id=1, replica_groups=mesh['grp'=8,'leaf'=32] {'leaf'}, use_global_device_ids=true, to_apply=%region_35.37 | all-reduce | flops 256 | bytes 2048 | tf_op jit(solution)/shard_map/psum | solution.py:129
  1630.3 10.7 all-gather.3
  1641.0 3.3 convolution_bitcast_fusion
  1644.3 1.9 fusion.168
  1647.5 77.5 %psum.95 = f32[]{:T(128)} all-reduce(f32[]{:T(128)} %multiply_reduce_fusion.1), channel_id=1, replica_groups=mesh['grp'=8,'leaf'=32] {'grp','leaf'}, use_global_device_ids=true, to_apply=%region_37.39 | all-reduce | flops 1 | bytes 8 | tf_op jit(solution)/shard_map/psum | solution.py:102
  (563 shorter events, 287.9 us)
Async XLA Ops:
  7.2 8.9 copy-start
  7.2 628.2 %reduce-scatter.5.cloned.1.call-start = ((), (), s32[]{:S(2)}) async-start(), calls=%async_computation.4 | async-start | bytes 135168 | tf_op jit(solution)/shard_map/reduce_scatter | solution.py:122
  9.9 6.2 copy-start.11
  9.9 6.2 copy-start.12
  17.2 4.9 collective-permute-start
  22.4 24.6 %collective-permute-start.1 = (bf16[2,2048,128]{2,1,0:T(8,128)(2,1)S(1)}, bf16[2,2048,128]{2,1,0:T(8,128)(2,1)}, u32[]{:S(2)}, u32[]{:S(2)}) collective-permute-start(bf16[2,2048,128]{2,1,0:T(8,128)(2,1)S(1)} %get-tuple-element.650), channel_id=1, source_target_pairs={{0,2},{1,3},{2,0},{3,1},{4,6},{5,7},{6,4},{7,5},{8,10},{9,11},{10,... | collective-permute-start | bytes 3145736 | tf_op jit(solution)/shard_map/ppermute | solution.py:24
  48.8 47.6 %collective-permute-start.2 = (bf16[4,2048,128]{2,1,0:T(8,128)(2,1)S(1)}, bf16[4,2048,128]{2,1,0:T(8,128)(2,1)}, u32[]{:S(2)}, u32[]{:S(2)}) collective-permute-start(bf16[4,2048,128]{2,1,0:T(8,128)(2,1)S(1)} %bitcast.453), channel_id=1, source_target_pairs={{0,4},{1,5},{2,6},{3,7},{4,0},{5,1},{6,2},{7,3},{8,12},{9,13},{10,... | collective-permute-start | bytes 6291464 | tf_op jit(solution)/shard_map/ppermute | solution.py:24
  101.2 90.3 %collective-permute-start.3 = (bf16[8,2048,128]{2,1,0:T(8,128)(2,1)}, bf16[8,2048,128]{2,1,0:T(8,128)(2,1)}, u32[]{:S(2)}, u32[]{:S(2)}) collective-permute-start(bf16[8,2048,128]{2,1,0:T(8,128)(2,1)} %bitcast.82), channel_id=1, source_target_pairs={{0,8},{1,9},{2,10},{3,11},{4,12},{5,13},{6,14},{7,15},{8,0},{9,1},... | collective-permute-start | bytes 12582920 | tf_op jit(solution)/shard_map/ppermute | solution.py:24
  198.9 12.5 copy-start.8
  198.9 12.6 copy-start.6
  198.9 12.6 copy-start.7
  198.9 12.7 copy-start.9
  198.9 213.6 %copy-start.10 = (s32[1,256]{1,0:T(1,128)S(1)}, s32[1,256]{1,0:T(1,128)}, u32[]{:S(2)}) copy-start(s32[1,256]{1,0:T(1,128)} %param.29) | copy-start | bytes 3076
  210.2 202.9 %collective-permute-start.4 = (bf16[16,2048,128]{2,1,0:T(8,128)(2,1)}, bf16[16,2048,128]{2,1,0:T(8,128)(2,1)}, u32[]{:S(2)}, u32[]{:S(2)}) collective-permute-start(bf16[16,2048,128]{2,1,0:T(8,128)(2,1)} %bitcast.447), channel_id=1, source_target_pairs={{0,16},{1,17},{2,18},{3,19},{4,20},{5,21},{6,22},{7,23},{8,24},{9,... | collective-permute-start | bytes 25165832 | tf_op jit(solution)/shard_map/ppermute | solution.py:24
  546.6 2.8 copy-start.2
  547.6 428.9 %reduce-scatter.7.cloned.1.call-start = ((), (), s32[]{:S(2)}) async-start(), calls=%async_computation.5 | async-start | bytes 135168 | tf_op jit(solution)/shard_map/reduce_scatter | solution.py:122
  895.2 416.3 %reduce-scatter.9.cloned.1.call-start = ((), (), s32[]{:S(2)}) async-start(), calls=%async_computation.6 | async-start | bytes 135168 | tf_op jit(solution)/shard_map/reduce_scatter | solution.py:122
  895.3 79.3 %copy-start.3 = (f32[2048,256]{1,0:T(8,128)S(1)}, f32[2048,256]{1,0:T(8,128)}, u32[]{:S(2)}) copy-start(f32[2048,256]{1,0:T(8,128)} %fusion.135) | copy-start | bytes 6291460
  1230.3 415.9 %reduce-scatter.11.cloned.1.call-start = ((), (), s32[]{:S(2)}) async-start(), calls=%async_computation.7 | async-start | bytes 135168 | tf_op jit(solution)/shard_map/reduce_scatter | solution.py:122
  1230.4 79.3 %copy-start.4 = (f32[2048,256]{1,0:T(8,128)S(1)}, f32[2048,256]{1,0:T(8,128)}, u32[]{:S(2)}) copy-start(f32[2048,256]{1,0:T(8,128)} %fusion.135) | copy-start | bytes 6291460
  1565.5 78.9 %copy-start.5 = (f32[2048,256]{1,0:T(8,128)S(1)}, f32[2048,256]{1,0:T(8,128)}, u32[]{:S(2)}) copy-start(f32[2048,256]{1,0:T(8,128)} %fusion.135) | copy-start | bytes 6291460
  1641.0 86.0 %copy-start.1 = (bf16[128,128]{1,0:T(8,128)(2,1)S(1)}, bf16[128,128]{1,0:T(8,128)(2,1)}, u32[]{:S(2)}) copy-start(bf16[128,128]{1,0:T(8,128)(2,1)} %param.24) | copy-start | bytes 98308
Sparse Core Ops, SparseCore 0:
  547.7 80.5 reduce-scatter.4
  895.3 73.2 reduce-scatter.6
  1230.4 73.2 reduce-scatter.8
  1565.6 73.5 reduce-scatter.10
